TPU v7x, 32 devices: a whole 2x2x4 slice. The times are simulated.
32 devices in a mesh: parts: 2 (over y), tm: 4 (over z), space: 2 (over x), spin: 2 (over core).
Axes of the slice: x: 2, y: 2, z: 4, core: 2. Of those that a mesh axis runs over, the one named last changes fastest.
Arguments:
- eigenvectors: float32 [2, 8, 3, 512, 256], P(None, ('parts', 'tm'), None, ('space', 'spin')), parts along dimension 1, may hold values from -0.25 to 0.25
- displaced: float32 [2, 3, 8, 3, 512, 256], P(None, None, ('parts', 'tm'), None, ('space', 'spin')), parts along dimension 2, may hold values from -0.25 to 0.25
- perambulators: float32 [2, 8, 4, 256, 256], P(None, 'parts', 'spin', 'space', 'tm'), parts along dimension 1, may hold values from -6 to 6
- gamma_values: float32 [2, 4, 4, 4], replicated, may hold values from -4 to 4
- spin_pattern: int32 [4, 4, 4], replicated, may hold values 0 or 1
- directions: int32 [4], replicated, may hold values from 0 to 2, as said below
- momenta: int32 [4], replicated, may hold values from 0 to 3
Outputs:
- products: float32 [2, 4, 8, 4, 256, 256], P(None, None, ('parts', 'tm'), 'spin', 'space'), parts along dimension 2
There are 2 independent parts, one for each index of `parts`. A program takes and returns all parts, laid end to end along the dimension named above; an argument that names none is the same for every part. Nothing has to cross between parts.
Inputs may be any that keep to these rules, and one draw needn't show every extreme that they name: Every one of the 3 directions is named by some operator.
All inputs are finite; a program needn't handle non-finite values.
Results may differ from a plain program's by a relative error of at most 0.0001.
Values sent between devices are 32-bit elements; how exact they have to be, the bound alone decides.
A program may use at most 64 MiB of HBM per device.

v0:
```python
import math

import jax
import jax.numpy as jnp
from jax import lax
from jax.sharding import PartitionSpec as P

highest = lax.Precision.HIGHEST


def local(eigenvectors, displaced, perambulators, gamma_values, spin_pattern, directions, momenta):
    time_dev = eigenvectors.shape[1]
    sites_dev = eigenvectors.shape[3]
    width = eigenvectors.shape[4]
    op_count = gamma_values.shape[1]
    spin_count = gamma_values.shape[2]
    sites_total = lax.axis_size(("space", "spin")) * sites_dev
    plane_sites = 2 * sites_dev
    extent = sites_total // plane_sites
    rows_dev = width // lax.axis_size("space")
    positions = lax.axis_index(("space", "spin")) * sites_dev + jnp.arange(
        sites_dev, dtype=jnp.int32
    )
    third = positions // plane_sites
    angles = (momenta[:, None] * third[None, :] % extent).astype(jnp.float32) * (
        2.0 * math.pi / extent
    )
    cosine = jnp.cos(angles)
    sine = jnp.sin(angles)
    tslice = 0
    lefts = [eigenvectors[:, tslice].reshape(-1, width)]
    columns = []
    for operator in range(op_count):
        moved = lax.dynamic_index_in_dim(displaced, directions[operator], 1, keepdims=False)[
            :, tslice
        ]
        cos_row = cosine[operator][:, None]
        sin_row = sine[operator][:, None]
        real_w = cos_row * moved[0] + sin_row * moved[1]
        imag_w = cos_row * moved[1] - sin_row * moved[0]
        block = jnp.concatenate(
            [jnp.stack([real_w, imag_w]), jnp.stack([imag_w, -real_w])], axis=-1
        )
        columns.append(block.reshape(-1, 2 * width))
    rights = [jnp.concatenate(columns, axis=1)]
    tslice = 0
    left_rows = lefts[tslice]
    pieces = lax.dot_general(
        left_rows,
        rights[tslice],
        (((0,), (0,)), ((), ())),
        precision=highest,
        preferred_element_type=jnp.float32,
    )
    quarter = lax.psum_scatter(pieces, ("space", "spin"), scatter_dimension=0, tiled=True)
    own_rows = lax.all_gather(quarter, "spin", axis=0, tiled=True)
    elementals = own_rows.reshape(rows_dev, time_dev, op_count, 2, width)
    spin_matrix = gamma_values * spin_pattern.astype(jnp.float32)[None]
    sink_dev = spin_count // lax.axis_size("spin")
    spin_rows = lax.dynamic_slice_in_dim(
        spin_matrix, lax.axis_index("spin") * sink_dev, sink_dev, 2
    )
    arrived = lax.all_to_all(perambulators, "tm", split_axis=1, concat_axis=4, tiled=True)
    arrived = lax.all_gather(arrived, "spin", axis=2, tiled=True)
    piece = lax.all_gather(arrived, "space", axis=3, tiled=True)
    real_q = jnp.einsum("oab,tbls->otals", spin_rows[0], piece[0], precision=highest) - jnp.einsum(
        "oab,tbls->otals", spin_rows[1], piece[1], precision=highest
    )
    imag_q = jnp.einsum("oab,tbls->otals", spin_rows[0], piece[1], precision=highest) + jnp.einsum(
        "oab,tbls->otals", spin_rows[1], piece[0], precision=highest
    )
    block = elementals
    real_e = block[:, :, :, 0]
    imag_e = block[:, :, :, 1]
    real_r = jnp.einsum("ktol,otals->otaks", real_e, real_q, precision=highest) - jnp.einsum(
        "ktol,otals->otaks", imag_e, imag_q, precision=highest
    )
    imag_r = jnp.einsum("ktol,otals->otaks", real_e, imag_q, precision=highest) + jnp.einsum(
        "ktol,otals->otaks", imag_e, real_q, precision=highest
    )
    return jnp.stack([real_r, imag_r])


def solution(mesh):
    in_specs = (
        P(None, ("parts", "tm"), None, ("space", "spin"), None),
        P(None, None, ("parts", "tm"), None, ("space", "spin"), None),
        P(None, "parts", "spin", "space", "tm"),
        P(),
        P(),
        P(),
        P(),
    )
    out_specs = P(None, None, ("parts", "tm"), "spin", "space", None)
    return jax.shard_map(local, mesh=mesh, in_specs=in_specs, out_specs=out_specs, check_vma=False)
```

profile of v0, /device:TPU:0, one launch (start us, length us, event | category | flops | bytes accessed | tf_op | source)
XLA Modules:
  0.0 136.4 jit_solution(16700542760090385622)
XLA Ops:
  7.4 2.0 %copy.47 = f32[2,4,2,128,64]{3,4,2,0,1:T(8,128)} copy(f32[2,4,2,128,64]{3,4,2,1,0:T(8,128)} %param.9) | data formatting | bytes 1048576 | tf_op args[2]
  9.3 6.3 %all-to-all-start = ((f32[2,4,2,128,64]{3,4,2,0,1:T(8,128)}), f32[2,4,2,128,64]{3,4,2,0,1:T(8,128)S(1)}, u32[]{:S(2)}, u32[]{:S(2)}) async-start(f32[2,4,2,128,64]{3,4,2,0,1:T(8,128)} %copy.47), calls=%async_computation | async-start | bytes 1048576 | tf_op jit(solution)/shard_map/all_to_all | solution.py:63
  15.7 0.7 fusion.31
  23.9 0.1 fusion.25
  24.0 4.0 %fusion.27 = (f32[1,3,128,256]{3,2,1,0:T(8,128)}, f32[1,3,128,256]{3,2,1,0:T(8,128)}, f32[1,3,128,256]{3,2,1,0:T(8,128)}, f32[1,3,128,256]{3,2,1,0:T(8,128)S(1)}...) fusion(f32[2,3,1,3,128,256]{5,4,3,2,1,0:T(8,128)} %param.8, ...), kind=kLoop, calls=%fused_computation.75 | loop fusion | flops 2752512 | bytes 7868436 | tf_op jit(solution)/shard_map/neg | solution.py:42
  28.0 2.2 %all-to-all-done = f32[2,4,2,128,64]{3,4,2,0,1:T(8,128)S(1)} async-done(((f32[2,4,2,128,64]{3,4,2,0,1:T(8,128)}), f32[2,4,2,128,64]{3,4,2,0,1:T(8,128)S(1)}, u32[]{:S(2)}, u32[]{:S(2)}) %all-to-all-start) | async-done | bytes 524320 | tf_op jit(solution)/shard_map/all_to_all | solution.py:63
  30.2 1.0 copy.49
  31.2 0.0 reduce-scatter.4.cloned.1.call-start
  31.3 1.6 %maximum_maximum_fusion = f32[2,3,128,512]{3,2,1,0:T(8,128)S(1)} fusion(f32[1,3,128,256]{3,2,1,0:T(8,128)} %get-tuple-element.5, f32[1,3,128,256]{3,2,1,0:T(8,128)} %get-tuple-element.13, f32[1,3,128,256]{3,2,1,0:T(8,128)} %get-tuple-element.6), kind=kLoop, calls=%fused_computation.12 | loop fusion | flops 1179648 | bytes 2752512 | tf_op jit(solution)/shard_map/concatenate | solution.py:41
  33.0 0.2 maximum_maximum_fusion.1
  33.2 0.2 maximum_maximum_fusion.2
  33.4 0.2 maximum_maximum_fusion.3
  33.5 10.6 %fusion.8 = f32[256,2048]{0,1:T(8,128)S(1)} fusion(f32[768,256]{1,0:T(8,128)S(1)} %bitcast.149, f32[768,512]{1,0:T(8,128)S(1)} %bitcast.158, f32[768,512]{1,0:T(8,128)S(1)} %bitcast.157, f32[768,512]{1,0:T(8,128)S(1)} %bitcast.156, f32[768,512]{1,0:T(8,128)S(1)} %bitcast.155), kind=kOutput, calls=%fused_computation.8 | convolution fusion | flops 4836556800 | bytes 9175040 | tf_op jit(solution)/shard_map/dot_general | solution.py:48
  44.1 1.8 %copy.78 = f32[256,2048]{1,0:T(8,128)} copy(f32[256,2048]{0,1:T(8,128)S(1)} %fusion.8) | data formatting | bytes 4194304
  46.0 0.0 all-gather.6.cloned.1.call-start
  46.1 2.9 %copy.50 = f32[2,1,4,128,256]{4,2,3,1,0:T(4,128)} copy(f32[2,1,4,128,256]{4,3,1,0,2:T(8,128)} %all-gather.4.cloned.1.call-done) | data formatting | bytes 2097152 | tf_op jit(solution)/shard_map/all_gather | solution.py:64
  49.0 0.2 all-gather.8.cloned.1.call-start
  49.3 44.3 %reduce-scatter.4.cloned.1.call-done = f32[64,2048]{1,0:T(8,128)} async-done(((f32[256,2048]{1,0:T(8,128)}), f32[64,2048]{1,0:T(8,128)}) %reduce-scatter.4.cloned.1.call-update) | async-done | bytes 524304 | tf_op jit(solution)/shard_map/reduce_scatter | solution.py:55
  93.6 0.0 all-gather.6.cloned.1.call-done
  93.6 4.1 %fusion.13 = f32[4,2,256,256]{3,0,2,1:T(4,128)S(1)} fusion(f32[2,1,4,256,256]{4,2,3,1,0:T(4,128)} %all-gather.6.cloned.1.call-done, f32[4,2,4,1]{2,1,0,3:T(2,128)S(1)} %get-tuple-element.27), kind=kOutput, calls=%fused_computation.22 | convolution fusion | flops 25165824 | bytes 3145856 | tf_op jit(solution)/shard_map/oab,tbls->otals/dot_general | solution.py:66
  97.8 4.5 %convolution_subtract_fusion = f32[4,2,256,256]{3,0,2,1:T(4,128)} fusion(f32[4,2,256,256]{3,0,2,1:T(4,128)S(1)} %fusion.13, f32[2,1,4,256,256]{4,2,3,1,0:T(4,128)S(1)} %copy-done.3, f32[4,2,4,1]{2,1,0,3:T(2,128)S(1)} %get-tuple-element.26), kind=kOutput, calls=%fused_computation.11 | convolution fusion | flops 25690112 | bytes 5246976 | tf_op jit(solution)/shard_map/oab,tbls->otals/dot_general | solution.py:66
  102.2 1.9 %copy.56 = f32[4,2,256,256]{2,3,1,0:T(8,128)S(1)} copy(f32[4,2,256,256]{3,0,2,1:T(4,128)} %convolution_subtract_fusion) | data formatting | bytes 4194304 | tf_op jit(solution)/shard_map/sub | solution.py:66
  104.2 4.1 %fusion.14 = f32[4,2,256,256]{3,0,2,1:T(4,128)S(1)} fusion(f32[2,1,4,256,256]{4,2,3,1,0:T(4,128)} %all-gather.6.cloned.1.call-done, f32[4,2,4,1]{2,1,0,3:T(2,128)S(1)} %get-tuple-element.27), kind=kOutput, calls=%fused_computation.23 | convolution fusion | flops 25165824 | bytes 3145856 | tf_op jit(solution)/shard_map/oab,tbls->otals/dot_general | solution.py:69
  108.3 4.5 %convolution_add_fusion = f32[4,2,256,256]{3,0,2,1:T(4,128)} fusion(f32[4,2,256,256]{3,0,2,1:T(4,128)S(1)} %fusion.14, f32[2,1,4,256,256]{4,2,3,1,0:T(4,128)S(1)} %copy-done.4, f32[4,2,4,1]{2,1,0,3:T(2,128)S(1)} %get-tuple-element.26), kind=kOutput, calls=%fused_computation.10 | convolution fusion | flops 25690112 | bytes 5246976 | tf_op jit(solution)/shard_map/oab,tbls->otals/dot_general | solution.py:69
  112.8 2.9 %copy.60 = f32[4,2,256,256]{2,3,1,0:T(8,128)} copy(f32[4,2,256,256]{3,0,2,1:T(4,128)} %convolution_add_fusion) | data formatting | bytes 4194304 | tf_op jit(solution)/shard_map/add | solution.py:69
  115.7 2.5 %copy.54 = f32[128,2048]{0,1:T(8,128)} copy(f32[128,2048]{1,0:T(8,128)} %all-gather.8.cloned.1.call-done) | data formatting | bytes 2097152 | tf_op jit(solution)/shard_map/all_gather | solution.py:56
  118.3 3.1 %fusion.16 = f32[4,2,256,128]{3,2,1,0:T(8,128)S(1)} fusion(f32[4,2,256,256]{2,3,1,0:T(8,128)S(1)} %copy.56, f32[128,1,4,2,256]{0,4,3,2,1:T(8,128)} %bitcast.150), kind=kOutput, calls=%fused_computation.27 | convolution fusion | flops 805306368 | bytes 3670016 | tf_op jit(solution)/shard_map/ktol,otals->otaks/dot_general | solution.py:75
  121.4 1.9 %fusion.15 = f32[4,2,256,128]{3,2,1,0:T(8,128)S(1)} fusion(f32[4,2,256,256]{2,3,1,0:T(8,128)S(1)} %copy-done.1, f32[128,1,4,2,256]{0,4,3,2,1:T(8,128)S(1)} %bitcast.151), kind=kOutput, calls=%fused_computation.26 | convolution fusion | flops 805306368 | bytes 3670016 | tf_op jit(solution)/shard_map/ktol,otals->otaks/dot_general | solution.py:78
  123.4 2.0 %fusion.12 = f32[1,4,1,2,128,256]{4,5,3,1,2,0:T(8,128)S(1)} fusion(f32[4,2,256,128]{3,2,1,0:T(8,128)S(1)} %fusion.16, f32[4,2,256,256]{2,3,1,0:T(8,128)S(1)} %copy-done.1, f32[128,1,4,2,256]{0,4,3,2,1:T(8,128)S(1)} %bitcast.152), kind=kOutput, calls=%fused_computation.19 | convolution fusion | flops 805568512 | bytes 4718592 | tf_op jit(solution)/shard_map/ktol,otals->otaks/dot_general | solution.py:75
  125.3 2.0 %fusion.11 = f32[1,4,1,2,128,256]{4,5,3,1,2,0:T(8,128)S(1)} fusion(f32[4,2,256,128]{3,2,1,0:T(8,128)S(1)} %fusion.15, f32[4,2,256,256]{2,3,1,0:T(8,128)S(1)} %copy.56, f32[128,1,4,2,256]{0,4,3,2,1:T(8,128)S(1)} %bitcast.153), kind=kOutput, calls=%fused_computation.17 | convolution fusion | flops 805568512 | bytes 4718592 | tf_op jit(solution)/shard_map/ktol,otals->otaks/dot_general | solution.py:78
  127.3 0.2 pad_maximum_fusion
  127.5 1.8 %copy.63 = f32[2,4,1,2,128,256]{5,4,3,2,1,0:T(8,128)} copy(f32[2,4,1,2,128,256]{4,5,3,1,2,0:T(8,128)S(1)} %pad_maximum_fusion) | data formatting | bytes 4194304 | tf_op jit(solution)/shard_map/stack | solution.py:81
  (42 shorter events, 0.2 us)
Async XLA Ops:
  7.4 26.2 %copy-start = (f32[2,1,3,128,256]{4,3,2,1,0:T(8,128)S(1)}, f32[2,1,3,128,256]{4,3,2,1,0:T(8,128)}, u32[]{:S(2)}) copy-start(f32[2,1,3,128,256]{4,3,2,1,0:T(8,128)} %param.7) | copy-start | bytes 2359300
  7.4 8.3 %copy-start.11 = (s32[4]{0:T(128)S(1)}, s32[4]{0:T(128)}, u32[]{:S(2)}) copy-start(s32[4]{0:T(128)} %param.12) | copy-start | bytes 52
  7.4 16.5 %copy-start.13 = (s32[4]{0:T(128)S(1)}, s32[4]{0:T(128)}, u32[]{:S(2)}) copy-start(s32[4]{0:T(128)} %param.13) | copy-start | bytes 52
  9.3 20.8 %all-to-all-start = ((f32[2,4,2,128,64]{3,4,2,0,1:T(8,128)}), f32[2,4,2,128,64]{3,4,2,0,1:T(8,128)S(1)}, u32[]{:S(2)}, u32[]{:S(2)}) async-start(f32[2,4,2,128,64]{3,4,2,0,1:T(8,128)} %copy.47), calls=%async_computation | async-start | bytes 1048576 | tf_op jit(solution)/shard_map/all_to_all | solution.py:63
  15.6 30.4 %all-gather.4.cloned.1.call-start = ((), (), s32[]{:S(2)}) async-start(), calls=%async_computation.2 | async-start | bytes 1572864 | tf_op jit(solution)/shard_map/all_gather | solution.py:64
  30.2 2.8 %copy-start.7 = (f32[1,3,128,256]{3,2,1,0:T(8,128)S(1)}, f32[1,3,128,256]{3,2,1,0:T(8,128)}, u32[]{:S(2)}) copy-start(f32[1,3,128,256]{3,2,1,0:T(8,128)} %get-tuple-element.23) | copy-start | bytes 1179652
  31.2 1.8 %copy-start.8 = (f32[1,3,128,256]{3,2,1,0:T(8,128)S(1)}, f32[1,3,128,256]{3,2,1,0:T(8,128)}, u32[]{:S(2)}) copy-start(f32[1,3,128,256]{3,2,1,0:T(8,128)} %get-tuple-element.24) | copy-start | bytes 1179652
  31.2 62.3 %reduce-scatter.4.cloned.1.call-start = ((), (), s32[]{:S(2)}) async-start(), calls=%async_computation.5 | async-start | bytes 2621440 | tf_op jit(solution)/shard_map/reduce_scatter | solution.py:55
  31.3 1.7 %copy-start.9 = (f32[1,3,128,256]{3,2,1,0:T(8,128)S(1)}, f32[1,3,128,256]{3,2,1,0:T(8,128)}, u32[]{:S(2)}) copy-start(f32[1,3,128,256]{3,2,1,0:T(8,128)} %get-tuple-element.25) | copy-start | bytes 1179652
  31.3 1.9 %copy-start.5 = (f32[1,3,128,256]{3,2,1,0:T(8,128)S(1)}, f32[1,3,128,256]{3,2,1,0:T(8,128)}, u32[]{:S(2)}) copy-start(f32[1,3,128,256]{3,2,1,0:T(8,128)} %get-tuple-element.21) | copy-start | bytes 1179652
  31.3 1.9 %copy-start.6 = (f32[1,3,128,256]{3,2,1,0:T(8,128)S(1)}, f32[1,3,128,256]{3,2,1,0:T(8,128)}, u32[]{:S(2)}) copy-start(f32[1,3,128,256]{3,2,1,0:T(8,128)} %get-tuple-element.22) | copy-start | bytes 1179652
  46.0 3.2 %copy-start.10 = (s32[4,4,4]{2,1,0:T(4,128)S(1)}, s32[4,4,4]{2,1,0:T(4,128)}, u32[]{:S(2)}) copy-start(s32[4,4,4]{2,1,0:T(4,128)} %param.11) | copy-start | bytes 772
  46.0 3.3 %copy-start.12 = (f32[2,4,4,4]{3,2,1,0:T(4,128)S(1)}, f32[2,4,4,4]{3,2,1,0:T(4,128)}, u32[]{:S(2)}) copy-start(f32[2,4,4,4]{3,2,1,0:T(4,128)} %param.10) | copy-start | bytes 1540
  46.0 47.6 %all-gather.6.cloned.1.call-start = ((), (), s32[]{:S(2)}) async-start(), calls=%async_computation.3 | async-start | bytes 3145728 | tf_op jit(solution)/shard_map/all_gather | solution.py:65
  49.0 66.8 %all-gather.8.cloned.1.call-start = ((), (), s32[]{:S(2)}) async-start(), calls=%async_computation.4 | async-start | bytes 1572864 | tf_op jit(solution)/shard_map/all_gather | solution.py:56
  93.6 4.1 %copy-start.3 = (f32[2,1,4,256,256]{4,2,3,1,0:T(4,128)S(1)}, f32[2,1,4,256,256]{4,2,3,1,0:T(4,128)}, u32[]{:S(2)}) copy-start(f32[2,1,4,256,256]{4,2,3,1,0:T(4,128)} %all-gather.6.cloned.1.call-done) | copy-start | bytes 6291460
  104.2 4.1 %copy-start.4 = (f32[2,1,4,256,256]{4,2,3,1,0:T(4,128)S(1)}, f32[2,1,4,256,256]{4,2,3,1,0:T(4,128)}, u32[]{:S(2)}) copy-start(f32[2,1,4,256,256]{4,2,3,1,0:T(4,128)} %all-gather.6.cloned.1.call-done) | copy-start | bytes 6291460
  118.3 3.1 %copy-start.1 = (f32[4,2,256,256]{2,3,1,0:T(8,128)S(1)}, f32[4,2,256,256]{2,3,1,0:T(8,128)}, u32[]{:S(2)}) copy-start(f32[4,2,256,256]{2,3,1,0:T(8,128)} %copy.60) | copy-start | bytes 6291460
  118.3 3.1 %copy-start.2 = (f32[128,2048]{0,1:T(8,128)S(1)}, f32[128,2048]{0,1:T(8,128)}, u32[]{:S(2)}) copy-start(f32[128,2048]{0,1:T(8,128)} %copy.54) | copy-start | bytes 3145732
Sparse Core Ops, SparseCore 0:
  31.4 8.3 all-gather.3
  49.1 32.6 all-gather.5
  93.7 9.0 all-gather.7
Sparse Core Ops, SparseCore 1:
  46.1 47.5 reduce-scatter.3
where the time goes:
time: 137 us; the launch traced here: 136 us
  waiting for transfers between devices  46.6 us (34%)
  matrix products  36.8 us (27%)
  between operations  22.4 us (16%)
  local copies, waits for them, and re-layouts  17.6 us (13%)
  starting transfers between devices  6.63 us (5%)
  other arithmetic  6.41 us (5%)
    reduce_scatter x1, waiting for transfers between devices, local(): lax.psum_scatter(pieces, ('space', 'spin'), scatter_dimension=0, tiled=True)  44.3 us
    dot_general x1, matrix products, local(): lax.dot_general(left_rows, rights[tslice], (((0,), (0,)), ((), ())), prec...  10.6 us
    all_to_all x1, starting transfers between devices, local(): lax.all_to_all(perambulators, 'tm', split_axis=1, concat_axis=4, tiled=True)  6.32 us
    dot_general x1, matrix products, local(): jnp.einsum('oab,tbls->otals', spin_rows[1], piece[0], precision=highest)  4.46 us
    dot_general x1, matrix products, local(): jnp.einsum('oab,tbls->otals', spin_rows[1], piece[1], precision=highest)  4.46 us
    dot_general x1, matrix products, local(): jnp.einsum('oab,tbls->otals', spin_rows[0], piece[0], precision=highest)  4.13 us
    dot_general x1, matrix products, local(): jnp.einsum('oab,tbls->otals', spin_rows[0], piece[1], precision=highest)  4.13 us
    neg x1, other arithmetic, local(): -real_w  3.97 us
  transfers between devices with their start and end apart: 5, of which 2 were waited for; matrix products, arithmetic and copies ran while one was open for 32% of the time, Pallas kernels for 0%

commit v1 on v0

v1 whole, which is shorter than its diff:
```python
import functools
import math

import jax
import jax.numpy as jnp
import numpy as np
from jax import lax
from jax.experimental import pallas as pl
from jax.experimental.pallas import tpu as pltpu
from jax.sharding import PartitionSpec as P

MESH = pl.DeviceIdType.MESH
f32 = jnp.float32
bf16 = jnp.bfloat16


def split(value):
    high = value.astype(bf16)
    return high, (value - high.astype(f32)).astype(bf16)


def dot3(a_high, a_low, b_high, b_low):
    dot = functools.partial(jnp.dot, preferred_element_type=f32)
    return dot(a_high, b_high) + (dot(a_high, b_low) + dot(a_low, b_high))


def turn(value, groups, by):
    if by == 0:
        return value
    width = value.shape[-1]
    cut = width // groups * by
    if width % 128 == 0:
        return pltpu.roll(value, width - cut, 1)
    return jnp.concatenate([value[:, cut:], value[:, :cut]], axis=1)


def table(index, values):
    result = f32(values[0])
    for j in range(1, len(values)):
        result = jnp.where(index == j, f32(values[j]), result)
    return result


def exchange(
    n_tm, n_space, n_spin,
    vec_hbm, dis_hbm, per_hbm, gamma, pattern, directions, momenta,
    y_ref,
    vec, dis, per, lhs_h, lhs_l, part, part_in, g_out, g_in,
    stage, slots, elem, elem_h, elem_l, w_h, w_l,
    load_sem, z_send, z_recv, x_send, x_recv, s_send, s_recv,
    gs_send, gs_recv, gx_send, gx_recv, e_send, e_recv,
):
    n_op = gamma.shape[1]
    n_dir = dis_hbm.shape[1]
    nb = per_hbm.shape[2]
    rows = part.shape[4]
    width = part.shape[5]
    l_rows = slots.shape[4]
    lanes = slots.shape[5]
    z = lax.axis_index("tm")
    x = lax.axis_index("space")
    c = lax.axis_index("spin")
    other = 1 - c

    def tm_peer(d):
        return {"tm": lax.rem(z + d, n_tm)}

    def x_peer(e):
        return {"space": lax.rem(x + e, n_space)}

    sibling = {"spin": other}

    loads = [pltpu.make_async_copy(per_hbm, per, load_sem.at[0])]
    loads.append(pltpu.make_async_copy(vec_hbm.at[:, 0], vec, load_sem.at[1]))
    for k in range(n_dir):
        loads.append(pltpu.make_async_copy(dis_hbm.at[:, k, 0], dis.at[k], load_sem.at[2 + k]))
    for load in loads:
        load.start()

    peers = [tm_peer(d) for d in range(1, n_tm)] + [x_peer(e) for e in range(1, n_space)] + [sibling]
    barrier = pltpu.get_barrier_semaphore()
    for peer in peers:
        pl.semaphore_signal(barrier, inc=1, device_id=peer, device_id_type=MESH)
    pl.semaphore_wait(barrier, len(peers))

    sent = []

    def send(src, dst, send_sem, recv_sem, peer):
        copy = pltpu.make_async_remote_copy(
            src_ref=src, dst_ref=dst, send_sem=send_sem, recv_sem=recv_sem,
            device_id=peer, device_id_type=MESH,
        )
        copy.start()
        sent.append(copy)
        return copy

    def packed(tslice, reim):
        return jnp.concatenate([per[reim, tslice, b] for b in range(nb)], axis=1)

    from_sibling = {}
    from_x = {}
    from_z = {}

    def forward_sibling(e, d):
        from_sibling[e, d] = send(
            slots.at[e, d, c], slots.at[e, d, c], s_send.at[e, d], s_recv.at[e, d], sibling
        )

    def forward_x(d):
        for e in range(1, n_space):
            from_x[e, d] = send(
                slots.at[0, d, c], slots.at[e, d, c], x_send.at[e, d], x_recv.at[e, d], x_peer(e)
            )

    loads[0].wait()
    for reim in range(2):
        slots[0, 0, c, reim] = packed(z, reim)
    forward_x(0)
    order = sorted(range(1, n_tm), key=lambda d: min(d, n_tm - d))
    for d in order:
        for reim in range(2):
            stage[d, reim] = packed(lax.rem(z + d, n_tm), reim)
        from_z[d] = send(stage.at[d], slots.at[0, d, c], z_send.at[d], z_recv.at[d], tm_peer(d))
    forward_sibling(0, 0)

    depth = lhs_h.shape[1]
    half = depth // 2
    loads[1].wait()
    turned = vec[...].reshape(depth, width).T
    high, low = split(turned)
    for ref, value in ((lhs_h, high), (lhs_l, low)):
        ref[:width] = value
        ref[width:, :half] = -value[:, half:]
        ref[width:, half:] = value[:, :half]
    from_part = []
    to_x = {}

    def reduce_part(k):
        from_part[k].wait_recv()
        for e in range(n_space):
            dest = lax.rem(x + e, n_space)
            total = part[k, c, dest] + part_in[k, dest]
            if e == 0:
                g_in[k, 0] = total
            else:
                g_out[k, e] = total
                to_x[k, e] = send(
                    g_out.at[k, e], g_in.at[k, e], gx_send.at[k, e], gx_recv.at[k, e], x_peer(e)
                )

    for k in range(n_dir):
        loads[2 + k].wait()
        r_high, r_low = split(dis[k].reshape(depth, width))
        sums = dot3(lhs_h[...], lhs_l[...], r_high, r_low)
        for xb in range(n_space):
            for cb in range(n_spin):
                first = (xb * n_spin + cb) * rows
                for reim in range(2):
                    start = reim * width + first
                    part[k, cb, xb, reim] = sums[start : start + rows]
        from_part.append(
            send(part.at[k, other], part_in.at[k], gs_send.at[k], gs_recv.at[k], sibling)
        )
        if k > 0:
            reduce_part(k - 1)
    reduce_part(n_dir - 1)

    lane = lax.broadcasted_iota(jnp.int32, (1, lanes), 1)
    cols = lanes // nb

    def mix(e, d):
        first = pl.multiple_of(lax.rem(x + (n_space - e), n_space) * l_rows, l_rows)

        def one(o, carry):
            q_re = jnp.zeros((l_rows, lanes), f32)
            q_im = jnp.zeros((l_rows, lanes), f32)
            for cb in range(n_spin):
                real = slots[e, d, cb, 0]
                imag = slots[e, d, cb, 1]
                for r in range(nb):
                    factors = []
                    for reim in range(2):
                        vector = jnp.zeros((1, lanes), f32)
                        for a in range(nb):
                            b = cb * nb + (a + r) % nb
                            row = c * nb + a
                            value = gamma[reim, o, row, b] * pattern[o, row, b].astype(f32)
                            if a == 0:
                                vector = jnp.full((1, lanes), value)
                            else:
                                vector = jnp.where(lane >= a * cols, value, vector)
                        factors.append(vector)
                    re_r = turn(real, nb, r)
                    im_r = turn(imag, nb, r)
                    q_re += factors[0] * re_r - factors[1] * im_r
                    q_im += factors[0] * im_r + factors[1] * re_r
            w_high, w_low = split(jnp.concatenate([q_re, q_im], axis=1))
            w_h[d, o, pl.ds(first, l_rows)] = w_high
            w_l[d, o, pl.ds(first, l_rows)] = w_low
            return carry

        lax.fori_loop(0, n_op, one, 0)

    def take_x(d):
        for e in range(1, n_space):
            from_x[e, d].wait_recv()
            forward_sibling(e, d)

    for d in order:
        from_z[d].wait_recv()
        forward_x(d)
        forward_sibling(0, d)
    take_x(0)
    for d in [0] + order:
        from_sibling[0, d].wait_recv()
        mix(0, d)
    for e in range(1, n_space):
        from_sibling[e, 0].wait_recv()
        mix(e, 0)

    for copy in to_x.values():
        copy.wait_recv()
    angles = np.arange(n_space, dtype=np.float32) * np.float32(2.0 * math.pi / n_space)
    cosines = [float(v) for v in np.cos(angles)]
    sines = [float(v) for v in np.sin(angles)]
    for o in range(n_op):
        e_re = jnp.zeros((rows, width), f32)
        e_im = jnp.zeros((rows, width), f32)
        way = directions[o]
        for e in range(n_space):
            plane = lax.rem(x + (n_space - e), n_space)
            step = lax.rem(momenta[o] * plane, n_space)
            cos_s = table(step, cosines)
            sin_s = table(step, sines)
            g_re = g_in[way, e, 0]
            g_im = g_in[way, e, 1]
            e_re += cos_s * g_re + sin_s * g_im
            e_im += cos_s * g_im - sin_s * g_re
        elem[c, o, 0] = e_re
        elem[c, o, 1] = e_im
    elem_copy = send(elem.at[c], elem.at[c], e_send.at[0], e_recv.at[0], sibling)
    k_rows = n_spin * rows
    elem_copy.wait_recv()
    for o in range(n_op):
        for reim in range(2):
            value = jnp.concatenate([elem[cb, o, reim] for cb in range(n_spin)], axis=0)
            high, low = split(value)
            elem_h[o, reim * k_rows : (reim + 1) * k_rows] = high
            elem_l[o, reim * k_rows : (reim + 1) * k_rows] = low

    def multiply(d):
        owner = lax.rem(z + (n_tm - d), n_tm)

        def one(o, carry):
            m = dot3(elem_h[o], elem_l[o], w_h[d, o], w_l[d, o])
            y_ref[0, o, owner] = m[:k_rows, :lanes] - m[k_rows:, lanes:]
            y_ref[1, o, owner] = m[:k_rows, lanes:] + m[k_rows:, :lanes]
            return carry

        lax.fori_loop(0, n_op, one, 0)

    multiply(0)
    before = None
    for d in order + [None]:
        if d is not None:
            take_x(d)
        if before is not None:
            for e in range(1, n_space):
                from_sibling[e, before].wait_recv()
                mix(e, before)
            multiply(before)
        before = d

    for copy in sent:
        copy.wait_send()


def arrange(y_ref, out_ref):
    owners = y_ref.shape[2]
    nb = out_ref.shape[3]
    cols = y_ref.shape[4] // nb
    for reim in range(y_ref.shape[0]):
        for a in range(nb):
            out_ref[reim, 0, 0, a] = jnp.concatenate(
                [y_ref[reim, 0, owner, :, a * cols : (a + 1) * cols] for owner in range(owners)], axis=1
            )


def local(n_tm, n_space, n_spin, eigenvectors, displaced, perambulators, gamma_values, spin_pattern, directions, momenta):
    _, _, colours, sites, width = eigenvectors.shape
    n_dir = displaced.shape[1]
    n_op = gamma_values.shape[1]
    _, _, nb, l_rows, cols = perambulators.shape
    rows = width // (n_space * n_spin)
    k_rows = width // n_space
    lanes = nb * cols
    depth = 2 * colours * sites
    dma = pltpu.SemaphoreType.DMA
    smem = pl.BlockSpec(memory_space=pltpu.SMEM)
    hbm = pl.BlockSpec(memory_space=pl.ANY)
    y = pl.pallas_call(
        functools.partial(exchange, n_tm, n_space, n_spin),
        out_shape=jax.ShapeDtypeStruct((2, n_op, n_tm, k_rows, lanes), f32),
        in_specs=[hbm, hbm, hbm, smem, smem, smem, smem],
        out_specs=pl.BlockSpec(memory_space=pltpu.VMEM),
        scratch_shapes=[
            pltpu.VMEM((2, colours, sites, width), f32),
            pltpu.VMEM((n_dir, 2, colours, sites, width), f32),
            pltpu.VMEM(perambulators.shape, f32),
            pltpu.VMEM((2 * width, depth), bf16),
            pltpu.VMEM((2 * width, depth), bf16),
            pltpu.VMEM((n_dir, n_spin, n_space, 2, rows, width), f32),
            pltpu.VMEM((n_dir, n_space, 2, rows, width), f32),
            pltpu.VMEM((n_dir, n_space, 2, rows, width), f32),
            pltpu.VMEM((n_dir, n_space, 2, rows, width), f32),
            pltpu.VMEM((n_tm, 2, l_rows, lanes), f32),
            pltpu.VMEM((n_space, n_tm, n_spin, 2, l_rows, lanes), f32),
            pltpu.VMEM((n_spin, n_op, 2, rows, width), f32),
            pltpu.VMEM((n_op, 2 * k_rows, width), bf16),
            pltpu.VMEM((n_op, 2 * k_rows, width), bf16),
            pltpu.VMEM((n_tm, n_op, width, 2 * lanes), bf16),
            pltpu.VMEM((n_tm, n_op, width, 2 * lanes), bf16),
            dma((2 + n_dir,)),
            dma((n_tm,)), dma((n_tm,)),
            dma((n_space, n_tm)), dma((n_space, n_tm)),
            dma((n_space, n_tm)), dma((n_space, n_tm)),
            dma((n_dir,)), dma((n_dir,)),
            dma((n_dir, n_space)), dma((n_dir, n_space)),
            dma((1,)), dma((1,)),
        ],
        compiler_params=pltpu.CompilerParams(
            collective_id=0, has_side_effects=True, vmem_limit_bytes=44 * 2**20
        ),
        name="exchange_and_multiply",
    )(eigenvectors, displaced, perambulators, gamma_values, spin_pattern, directions, momenta)
    return pl.pallas_call(
        arrange,
        grid=(n_op,),
        out_shape=jax.ShapeDtypeStruct((2, n_op, 1, nb, k_rows, n_tm * cols), f32),
        in_specs=[pl.BlockSpec((2, 1, n_tm, k_rows, lanes), lambda o: (0, o, 0, 0, 0))],
        out_specs=pl.BlockSpec((2, 1, 1, nb, k_rows, n_tm * cols), lambda o: (0, o, 0, 0, 0, 0)),
        compiler_params=pltpu.CompilerParams(vmem_limit_bytes=16 * 2**20),
        name="arrange",
    )(y)


def solution(mesh):
    in_specs = (
        P(None, ("parts", "tm"), None, ("space", "spin"), None),
        P(None, None, ("parts", "tm"), None, ("space", "spin"), None),
        P(None, "parts", "spin", "space", "tm"),
        P(),
        P(),
        P(),
        P(),
    )
    out_specs = P(None, None, ("parts", "tm"), "spin", "space", None)
    run = functools.partial(local, mesh.shape["tm"], mesh.shape["space"], mesh.shape["spin"])
    return jax.shard_map(run, mesh=mesh, in_specs=in_specs, out_specs=out_specs, check_vma=False)
```

time: 137 us -> 41.1 us (0.30)
  waiting for transfers between devices: 46.6 us -> 0 us
  matrix products: 36.8 us -> 0 us
  Pallas kernels: 0 us -> 34.9 us
  between operations: 22.4 us -> 0.04 us
  local copies, waits for them, and re-layouts: 17.6 us -> 5.84 us
  starting transfers between devices: 6.63 us -> 0 us
  other arithmetic: 6.41 us -> 0 us
    reduce_scatter x1 -> x0, waiting for transfers between devices: 44.3 us -> none  [local(): lax.psum_scatter(pieces, ('space', 'spin'), scatter_dimension=0, tiled=True)]
    dot_general x9 -> x0, matrix products: 36.8 us -> none  [the longest x1 10.6 us: local(): lax.dot_general(left_rows, rights[tslice], (((0,), (0,)), ((), ())), prec...]
    pallas_call x0 -> x2, Pallas kernels: none -> 34.9 us  [the longest x1 32.5 us: local(): pl.pallas_call(functools.partial(exchange, n_tm, n_space, n_spin), out_sh...]
    all_to_all x1 -> x0, starting transfers between devices: 6.32 us -> none  [local(): lax.all_to_all(perambulators, 'tm', split_axis=1, concat_axis=4, tiled=True)]
    all_gather x2 -> x0, local copies, waits for them, and re-layouts: 5.4 us -> none  [the longest x1 2.87 us: local(): arrived = lax.all_gather(arrived, 'spin', axis=2, tiled=True)]
    neg x1 -> x0, other arithmetic: 3.97 us -> none  [local(): -real_w]
    add x1 -> x0, local copies, waits for them, and re-layouts: 2.92 us -> none  [local(): jnp.einsum('oab,tbls->otals', spin_rows[0], piece[1], precision=highest)]
    all_to_all x1 -> x0, waiting for transfers between devices: 2.16 us -> none  [local(): lax.all_to_all(perambulators, 'tm', split_axis=1, concat_axis=4, tiled=True)]
  transfers between devices with their start and end apart: 5 -> 0, of which waited for: 2 -> 0; matrix products, arithmetic and copies ran while one was open for 32% -> 0% of each run, Pallas kernels for 0% -> 0%
where the time goes in v1:
time: 41.1 us; the launch traced here: 40.8 us
  Pallas kernels  34.9 us (85%)
  local copies, waits for them, and re-layouts  5.84 us (14%)
    pallas_call x1, Pallas kernels, local(): pl.pallas_call(functools.partial(exchange, n_tm, n_space, n_spin), out_sh...  32.5 us
    unnamed x13, local copies, waits for them, and re-layouts  5.84 us
    pallas_call x1, Pallas kernels, local(): pl.pallas_call(arrange, grid=(n_op,), out_shape=jax.ShapeDtypeStruct((2,...  2.34 us

profile of v1, /device:TPU:0, one launch (start us, length us, event | category | flops | bytes accessed | tf_op | source)
XLA Modules:
  0.0 40.8 jit_solution(50496082084414137)
XLA Ops:
  0.0 0.0 copy-start.1
  0.0 1.4 %copy.8.per_hbm = f32[2,4,2,128,64]{4,3,2,1,0:T(8,128)S(1)} copy(f32[2,4,2,128,64]{3,4,2,1,0:T(8,128)} %param.9) | data formatting | bytes 1048576 | tf_op args[2]
  1.5 0.0 copy-done.1
  1.5 0.0 copy-start
  1.5 1.7 %copy-done = f32[2,3,1,3,128,256]{5,4,3,2,1,0:T(8,128)S(1)} copy-done((f32[2,3,1,3,128,256]{5,4,3,2,1,0:T(8,128)S(1)}, f32[2,3,1,3,128,256]{5,4,3,2,1,0:T(8,128)}, u32[]{:S(2)}) %copy-start) | copy-done | bytes 2359320
  3.1 0.0 copy-start.2
  3.1 0.7 %copy-done.2 = f32[2,4,4,4]{3,2,1,0:T(4,128)S(1)} copy-done((f32[2,4,4,4]{3,2,1,0:T(4,128)S(1)}, f32[2,4,4,4]{3,2,1,0:T(4,128)}, u32[]{:S(2)}) %copy-start.2) | copy-done | bytes 536
  3.9 0.0 copy-start.3
  3.9 0.7 %copy-done.3 = s32[4,4,4]{2,1,0:T(4,128)S(1)} copy-done((s32[4,4,4]{2,1,0:T(4,128)S(1)}, s32[4,4,4]{2,1,0:T(4,128)}, u32[]{:S(2)}) %copy-start.3) | copy-done | bytes 280
  4.6 0.0 copy-start.4
  4.6 0.7 %copy-done.4 = s32[4]{0:T(128)S(1)} copy-done((s32[4]{0:T(128)S(1)}, s32[4]{0:T(128)}, u32[]{:S(2)}) %copy-start.4) | copy-done | bytes 40
  5.2 0.0 copy-start.5
  5.2 0.7 %copy-done.5 = s32[4]{0:T(128)S(1)} copy-done((s32[4]{0:T(128)S(1)}, s32[4]{0:T(128)}, u32[]{:S(2)}) %copy-start.5) | copy-done | bytes 40
  5.9 32.5 %exchange_and_multiply.1.y_ref = f32[2,4,4,128,128]{4,3,2,1,0:T(8,128)S(1)} custom-call(f32[2,1,3,128,256]{4,3,2,1,0:T(8,128)S(1)} %copy-done.1, f32[2,3,1,3,128,256]{5,4,3,2,1,0:T(8,128)S(1)} %copy-done, f32[2,4,2,128,64]{4,3,2,1,0:T(8,128)S(1)} %copy.8.per_hbm, f32[2,4,4,4]{3,2,1,0:T(4,128)S(1)} %copy-done.2, s32[4,4,4]{2,1,0:T(4,128)S(1)} %copy-done.3, ...), custom_call_target="tpu_custom_call" | custom-call | tf_op jit(solution)/shard_map/exchange_and_multiply/pallas_call | solution.py:301
  38.4 2.3 %arrange.1 = f32[2,4,1,2,128,256]{5,4,3,2,1,0:T(8,128)} custom-call(f32[2,4,4,128,128]{4,3,2,1,0:T(8,128)S(1)} %exchange_and_multiply.1.y_ref), custom_call_target="tpu_custom_call" | custom-call | tf_op jit(solution)/shard_map/arrange/pallas_call | solution.py:336
Async XLA Ops:
  0.0 1.5 %copy-start.1 = (f32[2,1,3,128,256]{4,3,2,1,0:T(8,128)S(1)}, f32[2,1,3,128,256]{4,3,2,1,0:T(8,128)}, u32[]{:S(2)}) copy-start(f32[2,1,3,128,256]{4,3,2,1,0:T(8,128)} %vec_hbm.1) | copy-start | bytes 2359300
  1.5 1.7 %copy-start = (f32[2,3,1,3,128,256]{5,4,3,2,1,0:T(8,128)S(1)}, f32[2,3,1,3,128,256]{5,4,3,2,1,0:T(8,128)}, u32[]{:S(2)}) copy-start(f32[2,3,1,3,128,256]{5,4,3,2,1,0:T(8,128)} %dis_hbm.1) | copy-start | bytes 7077892
  3.1 0.7 %copy-start.2 = (f32[2,4,4,4]{3,2,1,0:T(4,128)S(1)}, f32[2,4,4,4]{3,2,1,0:T(4,128)}, u32[]{:S(2)}) copy-start(f32[2,4,4,4]{3,2,1,0:T(4,128)} %gamma.1) | copy-start | bytes 1540
  3.9 0.7 %copy-start.3 = (s32[4,4,4]{2,1,0:T(4,128)S(1)}, s32[4,4,4]{2,1,0:T(4,128)}, u32[]{:S(2)}) copy-start(s32[4,4,4]{2,1,0:T(4,128)} %pattern.1) | copy-start | bytes 772
  4.6 0.7 %copy-start.4 = (s32[4]{0:T(128)S(1)}, s32[4]{0:T(128)}, u32[]{:S(2)}) copy-start(s32[4]{0:T(128)} %directions.1) | copy-start | bytes 52
  5.2 0.7 %copy-start.5 = (s32[4]{0:T(128)S(1)}, s32[4]{0:T(128)}, u32[]{:S(2)}) copy-start(s32[4]{0:T(128)} %momenta.1) | copy-start | bytes 52

commit v2 on v1

v2 whole, which is shorter than its diff:
```python
import functools
import math

import jax
import jax.numpy as jnp
import numpy as np
from jax import lax
from jax.experimental import pallas as pl
from jax.experimental.pallas import tpu as pltpu
from jax.sharding import PartitionSpec as P

MESH = pl.DeviceIdType.MESH
f32 = jnp.float32
bf16 = jnp.bfloat16


def split(value):
    high = value.astype(bf16)
    return high, (value - high.astype(f32)).astype(bf16)


def dot3(a_high, a_low, b_high, b_low, contract=0):
    dims = (((1,), (contract,)), ((), ()))
    dot = functools.partial(lax.dot_general, dimension_numbers=dims, preferred_element_type=f32)
    return dot(a_high, b_high) + (dot(a_high, b_low) + dot(a_low, b_high))


def table(index, values):
    result = f32(values[0])
    for j in range(1, len(values)):
        result = jnp.where(index == j, f32(values[j]), result)
    return result


def exchange(
    n_tm, n_space, n_spin,
    vec_hbm, dis_hbm, per_hbm, gamma_hbm, pattern_hbm, directions_hbm, momenta_hbm,
    out_ref,
    gamma, pattern, directions, momenta,
    vec, dis, lhs_h, lhs_l, part, part_in, g_out, g_in,
    slots, elem, elem_h, elem_l, w_h, w_l,
    load_sem, z_send, z_recv, x_send, x_recv, s_send, s_recv,
    gs_send, gs_recv, gx_send, gx_recv, e_send, e_recv,
):
    n_op = gamma.shape[1]
    n_dir = dis_hbm.shape[1]
    nb = per_hbm.shape[2]
    rows = part.shape[4]
    width = part.shape[5]
    cols = per_hbm.shape[3]
    lanes = nb * cols
    z = lax.axis_index("tm")
    x = lax.axis_index("space")
    c = lax.axis_index("spin")
    other = 1 - c

    def tm_peer(d):
        return {"tm": lax.rem(z + d, n_tm)}

    def x_peer(e):
        return {"space": lax.rem(x + e, n_space)}

    sibling = {"spin": other}

    own = pltpu.make_async_copy(per_hbm.at[:, z], slots.at[0, 0, c], load_sem.at[0])
    loads = [pltpu.make_async_copy(vec_hbm.at[:, 0], vec, load_sem.at[1])]
    for k in range(n_dir):
        loads.append(pltpu.make_async_copy(dis_hbm.at[:, k, 0], dis.at[k], load_sem.at[2 + k]))
    small = [(gamma_hbm, gamma), (pattern_hbm, pattern), (directions_hbm, directions), (momenta_hbm, momenta)]
    tables = [
        pltpu.make_async_copy(src, dst, load_sem.at[2 + n_dir + k]) for k, (src, dst) in enumerate(small)
    ]
    for load in loads + [own] + tables:
        load.start()

    peers = [tm_peer(d) for d in range(1, n_tm)] + [x_peer(e) for e in range(1, n_space)] + [sibling]
    barrier = pltpu.get_barrier_semaphore()
    for peer in peers:
        pl.semaphore_signal(barrier, inc=1, device_id=peer, device_id_type=MESH)
    pl.semaphore_wait(barrier, len(peers))

    sent = []

    def send(src, dst, send_sem, recv_sem, peer):
        copy = pltpu.make_async_remote_copy(
            src_ref=src, dst_ref=dst, send_sem=send_sem, recv_sem=recv_sem,
            device_id=peer, device_id_type=MESH,
        )
        copy.start()
        sent.append(copy)
        return copy

    from_sibling = {}
    from_x = {}
    from_z = {}

    def forward_sibling(e, d, src=None):
        from_sibling[e, d] = send(
            slots.at[e, d, c] if src is None else src, slots.at[e, d, c], s_send.at[e, d], s_recv.at[e, d], sibling
        )

    def forward_x(d, src=None):
        for e in range(1, n_space):
            from_x[e, d] = send(
                slots.at[0, d, c] if src is None else src, slots.at[e, d, c], x_send.at[e, d], x_recv.at[e, d], x_peer(e)
            )

    forward_x(0, per_hbm.at[:, z])
    order = sorted(range(1, n_tm), key=lambda d: min(d, n_tm - d))
    for d in order:
        from_z[d] = send(
            per_hbm.at[:, lax.rem(z + d, n_tm)], slots.at[0, d, c], z_send.at[d], z_recv.at[d], tm_peer(d)
        )
    forward_sibling(0, 0, per_hbm.at[:, z])

    depth = lhs_h.shape[1]
    half = depth // 2
    loads[0].wait()
    turned = vec[...].reshape(depth, width).T
    high, low = split(turned)
    for ref, value in ((lhs_h, high), (lhs_l, low)):
        ref[:width] = value
        ref[width:, :half] = -value[:, half:]
        ref[width:, half:] = value[:, :half]
    from_part = []
    to_x = {}

    def reduce_part(k):
        from_part[k].wait_recv()
        for e in range(n_space):
            dest = lax.rem(x + e, n_space)
            total = part[k, c, dest] + part_in[k, dest]
            if e == 0:
                g_in[k, 0] = total
            else:
                g_out[k, e] = total
                to_x[k, e] = send(
                    g_out.at[k, e], g_in.at[k, e], gx_send.at[k, e], gx_recv.at[k, e], x_peer(e)
                )

    def pass_on(d):
        from_z[d].wait_recv()
        forward_x(d)
        forward_sibling(0, d)

    for k in range(n_dir):
        loads[1 + k].wait()
        r_high, r_low = split(dis[k].reshape(depth, width))
        sums = dot3(lhs_h[...], lhs_l[...], r_high, r_low)
        for xb in range(n_space):
            for cb in range(n_spin):
                first = (xb * n_spin + cb) * rows
                for reim in range(2):
                    start = reim * width + first
                    part[k, cb, xb, reim] = sums[start : start + rows]
        from_part.append(
            send(part.at[k, other], part_in.at[k], gs_send.at[k], gs_recv.at[k], sibling)
        )
        if k > 0:
            reduce_part(k - 1)
        if k == 1:
            pass_on(order[0])
    reduce_part(n_dir - 1)
    for d in order[1:]:
        pass_on(d)

    def mix(e, d):
        block = lax.rem(x + (n_space - e), n_space)

        def one(o, carry):
            for a in range(nb):
                q_re = q_im = None
                row = c * nb + a
                for cb in range(n_spin):
                    for b in range(nb):
                        present = pattern[o, row, cb * nb + b].astype(f32)
                        s_re = gamma[0, o, row, cb * nb + b] * present
                        s_im = gamma[1, o, row, cb * nb + b] * present
                        real = slots[e, d, cb, 0, b]
                        imag = slots[e, d, cb, 1, b]
                        t_re = s_re * real - s_im * imag
                        t_im = s_re * imag + s_im * real
                        q_re = t_re if q_re is None else q_re + t_re
                        q_im = t_im if q_im is None else q_im + t_im
                for reim, value in ((0, q_re), (1, q_im)):
                    high, low = split(value)
                    first = reim * lanes + a * cols
                    w_h[d, o, block, first : first + cols] = high
                    w_l[d, o, block, first : first + cols] = low
            return carry

        lax.fori_loop(0, n_op, one, 0)

    def take_x(d):
        for e in range(1, n_space):
            from_x[e, d].wait_recv()
            forward_sibling(e, d)

    for copy in tables + [own]:
        copy.wait()
    take_x(0)
    for d in [0] + order:
        from_sibling[0, d].wait_recv()
        mix(0, d)
    for e in range(1, n_space):
        from_sibling[e, 0].wait_recv()
        mix(e, 0)

    for copy in to_x.values():
        copy.wait_recv()
    angles = np.arange(n_space, dtype=np.float32) * np.float32(2.0 * math.pi / n_space)
    cosines = [float(v) for v in np.cos(angles)]
    sines = [float(v) for v in np.sin(angles)]
    for o in range(n_op):
        e_re = jnp.zeros((rows, width), f32)
        e_im = jnp.zeros((rows, width), f32)
        way = directions[o]
        for e in range(n_space):
            plane = lax.rem(x + (n_space - e), n_space)
            step = lax.rem(momenta[o] * plane, n_space)
            cos_s = table(step, cosines)
            sin_s = table(step, sines)
            g_re = g_in[way, e, 0]
            g_im = g_in[way, e, 1]
            e_re += cos_s * g_re + sin_s * g_im
            e_im += cos_s * g_im - sin_s * g_re
        elem[c, o, 0] = e_re
        elem[c, o, 1] = e_im
    elem_copy = send(elem.at[c], elem.at[c], e_send.at[0], e_recv.at[0], sibling)
    k_rows = n_spin * rows
    elem_copy.wait_recv()
    for o in range(n_op):
        for reim in range(2):
            value = jnp.concatenate([elem[cb, o, reim] for cb in range(n_spin)], axis=0)
            high, low = split(value)
            elem_h[o, reim * k_rows : (reim + 1) * k_rows] = high
            elem_l[o, reim * k_rows : (reim + 1) * k_rows] = low

    tile = 128
    per_tile = tile // cols
    lane = lax.broadcasted_iota(jnp.int32, (k_rows, tile), 1)

    def multiply(d):
        owner = lax.rem(z + (n_tm - d), n_tm)
        place = lax.rem(owner, per_tile)
        held = (lane >= place * cols) & (lane < (place + 1) * cols)
        columns = pl.ds(pl.multiple_of(owner // per_tile * tile, tile), tile)

        def one(o, carry):
            right = [
                jnp.concatenate([w[d, o, block] for block in range(n_space)], axis=1) for w in (w_h, w_l)
            ]
            m = dot3(elem_h[o], elem_l[o], *right, contract=1)
            real = m[:k_rows, :lanes] - m[k_rows:, lanes:]
            imag = m[:k_rows, lanes:] + m[k_rows:, :lanes]
            for reim, value in ((0, real), (1, imag)):
                if lanes < tile:
                    value = jnp.concatenate([value, jnp.zeros((k_rows, tile - lanes), f32)], axis=1)
                for a in range(nb):
                    moved = pltpu.roll(value, lax.rem(place * cols + (tile - a * cols), tile), 1)
                    out_ref[reim, o, 0, a, :, columns] = jnp.where(
                        held, moved, out_ref[reim, o, 0, a, :, columns]
                    )
            return carry

        lax.fori_loop(0, n_op, one, 0)

    multiply(0)
    before = None
    for d in order + [None]:
        if d is not None:
            take_x(d)
        if before is not None:
            for e in range(1, n_space):
                from_sibling[e, before].wait_recv()
                mix(e, before)
            multiply(before)
        before = d

    for copy in sent:
        copy.wait_send()


def local(n_tm, n_space, n_spin, eigenvectors, displaced, perambulators, gamma_values, spin_pattern, directions, momenta):
    _, _, colours, sites, width = eigenvectors.shape
    n_dir = displaced.shape[1]
    n_op = gamma_values.shape[1]
    perambulators = jnp.swapaxes(perambulators, 3, 4)
    _, _, nb, cols, l_rows = perambulators.shape
    rows = width // (n_space * n_spin)
    k_rows = width // n_space
    lanes = nb * cols
    depth = 2 * colours * sites
    operands = (eigenvectors, displaced, perambulators, gamma_values, spin_pattern, directions, momenta)
    dma = pltpu.SemaphoreType.DMA
    smem = pltpu.SMEM
    hbm = pl.BlockSpec(memory_space=pltpu.HBM)
    return pl.pallas_call(
        functools.partial(exchange, n_tm, n_space, n_spin),
        out_shape=pltpu.VMEM((2, n_op, 1, nb, k_rows, n_tm * cols), f32),
        in_specs=[hbm] * 7,
        out_specs=pl.BlockSpec(memory_space=pltpu.VMEM),
        scratch_shapes=[
            smem(gamma_values.shape, f32),
            smem(spin_pattern.shape, jnp.int32),
            smem(directions.shape, jnp.int32),
            smem(momenta.shape, jnp.int32),
            pltpu.VMEM((2, colours, sites, width), f32),
            pltpu.VMEM((n_dir, 2, colours, sites, width), f32),
            pltpu.VMEM((2 * width, depth), bf16),
            pltpu.VMEM((2 * width, depth), bf16),
            pltpu.VMEM((n_dir, n_spin, n_space, 2, rows, width), f32),
            pltpu.VMEM((n_dir, n_space, 2, rows, width), f32),
            pltpu.VMEM((n_dir, n_space, 2, rows, width), f32),
            pltpu.VMEM((n_dir, n_space, 2, rows, width), f32),
            pltpu.VMEM((n_space, n_tm, n_spin, 2, nb, cols, l_rows), f32),
            pltpu.VMEM((n_spin, n_op, 2, rows, width), f32),
            pltpu.VMEM((n_op, 2 * k_rows, width), bf16),
            pltpu.VMEM((n_op, 2 * k_rows, width), bf16),
            pltpu.VMEM((n_tm, n_op, n_space, 2 * lanes, l_rows), bf16),
            pltpu.VMEM((n_tm, n_op, n_space, 2 * lanes, l_rows), bf16),
            dma((6 + n_dir,)),
            dma((n_tm,)), dma((n_tm,)),
            dma((n_space, n_tm)), dma((n_space, n_tm)),
            dma((n_space, n_tm)), dma((n_space, n_tm)),
            dma((n_dir,)), dma((n_dir,)),
            dma((n_dir, n_space)), dma((n_dir, n_space)),
            dma((1,)), dma((1,)),
        ],
        compiler_params=pltpu.CompilerParams(
            collective_id=0, has_side_effects=True, vmem_limit_bytes=48 * 2**20
        ),
        name="exchange_and_multiply",
    )(*[pltpu.with_memory_space_constraint(v, pltpu.HBM) for v in operands])


def solution(mesh):
    in_specs = (
        P(None, ("parts", "tm"), None, ("space", "spin"), None),
        P(None, None, ("parts", "tm"), None, ("space", "spin"), None),
        P(None, "parts", "spin", "space", "tm"),
        P(),
        P(),
        P(),
        P(),
    )
    out_specs = P(None, None, ("parts", "tm"), "spin", "space", None)
    run = functools.partial(local, mesh.shape["tm"], mesh.shape["space"], mesh.shape["spin"])
    return jax.shard_map(run, mesh=mesh, in_specs=in_specs, out_specs=out_specs, check_vma=False)
```

time: 41.1 us -> 35.1 us (0.85)
  the two profiles are of different devices: /device:TPU:0 before, /device:TPU:20 now
where the time goes in v2:
time: 35.1 us; the launch traced here: 34.9 us
  Pallas kernels  33.6 us (96%)
  local copies, waits for them, and re-layouts  1.32 us (4%)
    pallas_call x1, Pallas kernels, local(): pl.pallas_call(functools.partial(exchange, n_tm, n_space, n_spin), out_sh...  33.6 us
    unnamed x1, local copies, waits for them, and re-layouts  1.32 us

profile of v2, /device:TPU:20, one launch (start us, length us, event | category | flops | bytes accessed | tf_op | source)
XLA Modules:
  0.0 34.9 jit_solution(12018587155262284464)
XLA Ops:
  0.0 33.6 %exchange_and_multiply.1 = f32[2,4,1,2,128,256]{5,4,3,2,1,0:T(8,128)S(1)} custom-call(f32[2,1,3,128,256]{4,3,2,1,0:T(8,128)} %vec_hbm.1, f32[2,3,1,3,128,256]{5,4,3,2,1,0:T(8,128)} %dis_hbm.1, f32[2,4,2,64,128]{4,3,2,1,0:T(8,128)} %bitcast.1, f32[2,4,4,4]{3,2,1,0:T(4,128)} %gamma_hbm.1, s32[4,4,4]{2,1,0:T(4,128)} %pattern_hbm.1, s32[4]{0:T(128)} %directions_hbm.1, ...), custom_call_target="tpu_custom_call" | custom-call | tf_op jit(solution)/shard_map/exchange_and_multiply/pallas_call | solution.py:298
  33.6 1.3 %copy.9 = f32[2,4,1,2,128,256]{5,4,3,2,1,0:T(8,128)} copy(f32[2,4,1,2,128,256]{5,4,3,2,1,0:T(8,128)S(1)} %exchange_and_multiply.1) | data formatting | bytes 4194304

commit v3 on v2

--- a/solution.py
+++ b/solution.py
@@ -73,7 +73,14 @@
     for load in loads + [own] + tables:
         load.start()
 
-    peers = [tm_peer(d) for d in range(1, n_tm)] + [x_peer(e) for e in range(1, n_space)] + [sibling]
+    order = sorted(range(1, n_tm), key=lambda d: min(d, n_tm - d))
+    straight = order[:1]
+
+    def both_peer(e, d):
+        return {**tm_peer(d), **x_peer(e)}
+
+    peers = [both_peer(n_space - e, n_tm - d) for d in straight for e in range(1, n_space)]
+    peers += [tm_peer(d) for d in range(1, n_tm)] + [x_peer(e) for e in range(1, n_space)] + [sibling]
     barrier = pltpu.get_barrier_semaphore()
     for peer in peers:
         pl.semaphore_signal(barrier, inc=1, device_id=peer, device_id_type=MESH)
@@ -106,11 +113,16 @@
             )
 
     forward_x(0, per_hbm.at[:, z])
-    order = sorted(range(1, n_tm), key=lambda d: min(d, n_tm - d))
     for d in order:
         from_z[d] = send(
             per_hbm.at[:, lax.rem(z + d, n_tm)], slots.at[0, d, c], z_send.at[d], z_recv.at[d], tm_peer(d)
         )
+        if d in straight:
+            for e in range(1, n_space):
+                from_x[e, d] = send(
+                    per_hbm.at[:, lax.rem(z + d, n_tm)], slots.at[e, d, c],
+                    x_send.at[e, d], x_recv.at[e, d], both_peer(e, d),
+                )
     forward_sibling(0, 0, per_hbm.at[:, z])
 
     depth = lhs_h.shape[1]
@@ -140,7 +152,8 @@
 
     def pass_on(d):
         from_z[d].wait_recv()
-        forward_x(d)
+        if d not in straight:
+            forward_x(d)
         forward_sibling(0, d)
 
     for k in range(n_dir):
@@ -164,29 +177,31 @@
     for d in order[1:]:
         pass_on(d)
 
+    def mix_one(e, d, o):
+        block = lax.rem(x + (n_space - e), n_space)
+        for a in range(nb):
+            q_re = q_im = None
+            row = c * nb + a
+            for cb in range(n_spin):
+                for b in range(nb):
+                    present = pattern[o, row, cb * nb + b].astype(f32)
+                    s_re = gamma[0, o, row, cb * nb + b] * present
+                    s_im = gamma[1, o, row, cb * nb + b] * present
+                    real = slots[e, d, cb, 0, b]
+                    imag = slots[e, d, cb, 1, b]
+                    t_re = s_re * real - s_im * imag
+                    t_im = s_re * imag + s_im * real
+                    q_re = t_re if q_re is None else q_re + t_re
+                    q_im = t_im if q_im is None else q_im + t_im
+            for reim, value in ((0, q_re), (1, q_im)):
+                high, low = split(value)
+                first = reim * lanes + a * cols
+                w_h[d, o, block, first : first + cols] = high
+                w_l[d, o, block, first : first + cols] = low
+
     def mix(e, d):
-        block = lax.rem(x + (n_space - e), n_space)
-
         def one(o, carry):
-            for a in range(nb):
-                q_re = q_im = None
-                row = c * nb + a
-                for cb in range(n_spin):
-                    for b in range(nb):
-                        present = pattern[o, row, cb * nb + b].astype(f32)
-                        s_re = gamma[0, o, row, cb * nb + b] * present
-                        s_im = gamma[1, o, row, cb * nb + b] * present
-                        real = slots[e, d, cb, 0, b]
-                        imag = slots[e, d, cb, 1, b]
-                        t_re = s_re * real - s_im * imag
-                        t_im = s_re * imag + s_im * real
-                        q_re = t_re if q_re is None else q_re + t_re
-                        q_im = t_im if q_im is None else q_im + t_im
-                for reim, value in ((0, q_re), (1, q_im)):
-                    high, low = split(value)
-                    first = reim * lanes + a * cols
-                    w_h[d, o, block, first : first + cols] = high
-                    w_l[d, o, block, first : first + cols] = low
+            mix_one(e, d, o)
             return carry
 
         lax.fori_loop(0, n_op, one, 0)
@@ -240,13 +255,15 @@
     per_tile = tile // cols
     lane = lax.broadcasted_iota(jnp.int32, (k_rows, tile), 1)
 
-    def multiply(d):
+    def multiply(d, fresh=()):
         owner = lax.rem(z + (n_tm - d), n_tm)
         place = lax.rem(owner, per_tile)
         held = (lane >= place * cols) & (lane < (place + 1) * cols)
         columns = pl.ds(pl.multiple_of(owner // per_tile * tile, tile), tile)
 
-        def one(o, carry):
+        for o in range(n_op):
+            for e in fresh:
+                mix_one(e, d, o)
             right = [
                 jnp.concatenate([w[d, o, block] for block in range(n_space)], axis=1) for w in (w_h, w_l)
             ]
@@ -261,9 +278,6 @@
                     out_ref[reim, o, 0, a, :, columns] = jnp.where(
                         held, moved, out_ref[reim, o, 0, a, :, columns]
                     )
-            return carry
-
-        lax.fori_loop(0, n_op, one, 0)
 
     multiply(0)
     before = None
@@ -273,8 +287,7 @@
         if before is not None:
             for e in range(1, n_space):
                 from_sibling[e, before].wait_recv()
-                mix(e, before)
-            multiply(before)
+            multiply(before, range(1, n_space))
         before = d
 
     for copy in sent:

time: 35.1 us -> 32.6 us (0.929)
  the two profiles are of different devices: /device:TPU:20 before, /device:TPU:0 now
where the time goes in v3:
time: 32.6 us; the launch traced here: 32.5 us
  Pallas kernels  31.1 us (95%)
  local copies, waits for them, and re-layouts  1.32 us (4%)
    pallas_call x1, Pallas kernels, local(): pl.pallas_call(functools.partial(exchange, n_tm, n_space, n_spin), out_sh...  31.1 us
    unnamed x1, local copies, waits for them, and re-layouts  1.32 us

profile of v3, /device:TPU:0, one launch (start us, length us, event | category | flops | bytes accessed | tf_op | source)
XLA Modules:
  0.0 32.5 jit_solution(5039936580976766156)
XLA Ops:
  0.0 31.1 %exchange_and_multiply.1 = f32[2,4,1,2,128,256]{5,4,3,2,1,0:T(8,128)S(1)} custom-call(f32[2,1,3,128,256]{4,3,2,1,0:T(8,128)} %vec_hbm.1, f32[2,3,1,3,128,256]{5,4,3,2,1,0:T(8,128)} %dis_hbm.1, f32[2,4,2,64,128]{4,3,2,1,0:T(8,128)} %bitcast.1, f32[2,4,4,4]{3,2,1,0:T(4,128)} %gamma_hbm.1, s32[4,4,4]{2,1,0:T(4,128)} %pattern_hbm.1, s32[4]{0:T(128)} %directions_hbm.1, ...), custom_call_target="tpu_custom_call" | custom-call | tf_op jit(solution)/shard_map/exchange_and_multiply/pallas_call | solution.py:311
  31.2 1.3 %copy.9 = f32[2,4,1,2,128,256]{5,4,3,2,1,0:T(8,128)} copy(f32[2,4,1,2,128,256]{5,4,3,2,1,0:T(8,128)S(1)} %exchange_and_multiply.1) | data formatting | bytes 4194304

commit v4 on v3

--- a/solution.py
+++ b/solution.py
@@ -25,6 +25,28 @@
     return dot(a_high, b_high) + (dot(a_high, b_low) + dot(a_low, b_high))
 
 
+def block_product(o, owner, elem_h, elem_l, rights, before, after):
+    nb, k_rows = before.shape[3:5]
+    lanes = rights[0].shape[2] // 2
+    cols = lanes // nb
+    tile = 128
+    per_tile = tile // cols
+    lane = lax.broadcasted_iota(jnp.int32, (k_rows, tile), 1)
+    place = lax.rem(owner, per_tile)
+    held = (lane >= place * cols) & (lane < (place + 1) * cols)
+    columns = pl.ds(pl.multiple_of(owner // per_tile * tile, tile), tile)
+    right = [jnp.concatenate([w[o, block] for block in range(w.shape[1])], axis=1) for w in rights]
+    m = dot3(elem_h[o], elem_l[o], *right, contract=1)
+    real = m[:k_rows, :lanes] - m[k_rows:, lanes:]
+    imag = m[:k_rows, lanes:] + m[k_rows:, :lanes]
+    for reim, value in ((0, real), (1, imag)):
+        if lanes < tile:
+            value = jnp.concatenate([value, jnp.zeros((k_rows, tile - lanes), f32)], axis=1)
+        for a in range(nb):
+            moved = pltpu.roll(value, lax.rem(place * cols + (tile - a * cols), tile), 1)
+            after[reim, o, 0, a, :, columns] = jnp.where(held, moved, before[reim, o, 0, a, :, columns])
+
+
 def table(index, values):
     result = f32(values[0])
     for j in range(1, len(values)):
@@ -35,10 +57,10 @@
 def exchange(
     n_tm, n_space, n_spin,
     vec_hbm, dis_hbm, per_hbm, gamma_hbm, pattern_hbm, directions_hbm, momenta_hbm,
-    out_ref,
+    out_ref, elem_h, elem_l, last_h, last_l,
     gamma, pattern, directions, momenta,
     vec, dis, lhs_h, lhs_l, part, part_in, g_out, g_in,
-    slots, elem, elem_h, elem_l, w_h, w_l,
+    slots, elem, w_h, w_l,
     load_sem, z_send, z_recv, x_send, x_recv, s_send, s_recv,
     gs_send, gs_recv, gx_send, gx_recv, e_send, e_recv,
 ):
@@ -177,7 +199,9 @@
     for d in order[1:]:
         pass_on(d)
 
-    def mix_one(e, d, o):
+    def mix_one(e, d, o, to_h=None, to_l=None):
+        to_h = w_h.at[d] if to_h is None else to_h
+        to_l = w_l.at[d] if to_l is None else to_l
         block = lax.rem(x + (n_space - e), n_space)
         for a in range(nb):
             q_re = q_im = None
@@ -196,12 +220,12 @@
             for reim, value in ((0, q_re), (1, q_im)):
                 high, low = split(value)
                 first = reim * lanes + a * cols
-                w_h[d, o, block, first : first + cols] = high
-                w_l[d, o, block, first : first + cols] = low
+                to_h[o, block, first : first + cols] = high
+                to_l[o, block, first : first + cols] = low
 
     def mix(e, d):
         def one(o, carry):
-            mix_one(e, d, o)
+            mix_one(e, d, o, *((last_h, last_l) if d == order[-1] else ()))
             return carry
 
         lax.fori_loop(0, n_op, one, 0)
@@ -251,47 +275,50 @@
             elem_h[o, reim * k_rows : (reim + 1) * k_rows] = high
             elem_l[o, reim * k_rows : (reim + 1) * k_rows] = low
 
-    tile = 128
-    per_tile = tile // cols
-    lane = lax.broadcasted_iota(jnp.int32, (k_rows, tile), 1)
-
-    def multiply(d, fresh=()):
+    def multiply(d, unroll):
         owner = lax.rem(z + (n_tm - d), n_tm)
-        place = lax.rem(owner, per_tile)
-        held = (lane >= place * cols) & (lane < (place + 1) * cols)
-        columns = pl.ds(pl.multiple_of(owner // per_tile * tile, tile), tile)
-
-        for o in range(n_op):
-            for e in fresh:
-                mix_one(e, d, o)
-            right = [
-                jnp.concatenate([w[d, o, block] for block in range(n_space)], axis=1) for w in (w_h, w_l)
-            ]
-            m = dot3(elem_h[o], elem_l[o], *right, contract=1)
-            real = m[:k_rows, :lanes] - m[k_rows:, lanes:]
-            imag = m[:k_rows, lanes:] + m[k_rows:, :lanes]
-            for reim, value in ((0, real), (1, imag)):
-                if lanes < tile:
-                    value = jnp.concatenate([value, jnp.zeros((k_rows, tile - lanes), f32)], axis=1)
-                for a in range(nb):
-                    moved = pltpu.roll(value, lax.rem(place * cols + (tile - a * cols), tile), 1)
-                    out_ref[reim, o, 0, a, :, columns] = jnp.where(
-                        held, moved, out_ref[reim, o, 0, a, :, columns]
-                    )
-
-    multiply(0)
+
+        def one(o, carry):
+            for e in range(1, n_space):
+                if d > 0:
+                    mix_one(e, d, o)
+            block_product(o, owner, elem_h, elem_l, (w_h.at[d], w_l.at[d]), out_ref, out_ref)
+            return carry
+
+        if unroll:
+            for o in range(n_op):
+                one(o, 0)
+        else:
+            lax.fori_loop(0, n_op, one, 0)
+
+    multiply(0, False)
     before = None
-    for d in order + [None]:
-        if d is not None:
-            take_x(d)
+    for d in order:
+        take_x(d)
         if before is not None:
             for e in range(1, n_space):
                 from_sibling[e, before].wait_recv()
-            multiply(before, range(1, n_space))
+            multiply(before, d == order[-1])
         before = d
-
+    for e in range(1, n_space):
+        from_sibling[e, before].wait_recv()
+        for o in range(n_op):
+            mix_one(e, before, o, last_h, last_l)
     for copy in sent:
         copy.wait_send()
+
+
+def finish(n_tm, y_ref, elem_h, elem_l, last_h, last_l, out_hbm, whole, out_sem):
+    order = sorted(range(1, n_tm), key=lambda d: min(d, n_tm - d))
+    owner = lax.rem(lax.axis_index("tm") + (n_tm - order[-1]), n_tm)
+    copies = []
+    for o in range(y_ref.shape[1]):
+        whole[:, o] = y_ref[:, o]
+        block_product(o, owner, elem_h, elem_l, (last_h, last_l), y_ref, whole)
+        copies.append(pltpu.make_async_copy(whole.at[:, o], out_hbm.at[:, o], out_sem.at[o]))
+        copies[-1].start()
+    for copy in copies:
+        copy.wait()
 
 
 def local(n_tm, n_space, n_spin, eigenvectors, displaced, perambulators, gamma_values, spin_pattern, directions, momenta):
@@ -305,14 +332,21 @@
     lanes = nb * cols
     depth = 2 * colours * sites
     operands = (eigenvectors, displaced, perambulators, gamma_values, spin_pattern, directions, momenta)
+    out_dims = (2, n_op, 1, nb, k_rows, n_tm * cols)
     dma = pltpu.SemaphoreType.DMA
     smem = pltpu.SMEM
     hbm = pl.BlockSpec(memory_space=pltpu.HBM)
-    return pl.pallas_call(
+    y, *factors = pl.pallas_call(
         functools.partial(exchange, n_tm, n_space, n_spin),
-        out_shape=pltpu.VMEM((2, n_op, 1, nb, k_rows, n_tm * cols), f32),
+        out_shape=[
+            pltpu.VMEM(out_dims, f32),
+            pltpu.VMEM((n_op, 2 * k_rows, width), bf16),
+            pltpu.VMEM((n_op, 2 * k_rows, width), bf16),
+            pltpu.VMEM((n_op, n_space, 2 * lanes, l_rows), bf16),
+            pltpu.VMEM((n_op, n_space, 2 * lanes, l_rows), bf16),
+        ],
         in_specs=[hbm] * 7,
-        out_specs=pl.BlockSpec(memory_space=pltpu.VMEM),
+        out_specs=[pl.BlockSpec(memory_space=pltpu.VMEM)] * 5,
         scratch_shapes=[
             smem(gamma_values.shape, f32),
             smem(spin_pattern.shape, jnp.int32),
@@ -328,8 +362,6 @@
             pltpu.VMEM((n_dir, n_space, 2, rows, width), f32),
             pltpu.VMEM((n_space, n_tm, n_spin, 2, nb, cols, l_rows), f32),
             pltpu.VMEM((n_spin, n_op, 2, rows, width), f32),
-            pltpu.VMEM((n_op, 2 * k_rows, width), bf16),
-            pltpu.VMEM((n_op, 2 * k_rows, width), bf16),
             pltpu.VMEM((n_tm, n_op, n_space, 2 * lanes, l_rows), bf16),
             pltpu.VMEM((n_tm, n_op, n_space, 2 * lanes, l_rows), bf16),
             dma((6 + n_dir,)),
@@ -345,6 +377,15 @@
         ),
         name="exchange_and_multiply",
     )(*[pltpu.with_memory_space_constraint(v, pltpu.HBM) for v in operands])
+    return pl.pallas_call(
+        functools.partial(finish, n_tm),
+        out_shape=jax.ShapeDtypeStruct(out_dims, f32),
+        in_specs=[pl.BlockSpec(memory_space=pltpu.VMEM)] * 5,
+        out_specs=pl.BlockSpec(memory_space=pltpu.HBM),
+        scratch_shapes=[pltpu.VMEM(out_dims, f32), dma((n_op,))],
+        compiler_params=pltpu.CompilerParams(vmem_limit_bytes=32 * 2**20),
+        name="last_block",
+    )(y, *factors)
 
 
 def solution(mesh):

time: 32.6 us -> 33.8 us (1.037)
  Pallas kernels: 31.1 us -> 33.7 us
  local copies, waits for them, and re-layouts: 1.32 us -> 0 us
    pallas_call x0 -> x1, Pallas kernels: none -> 1.96 us  [local(): pl.pallas_call(functools.partial(finish, n_tm), out_shape=jax.ShapeDtypeS...]
    unnamed x1 -> x0, local copies, waits for them, and re-layouts: 1.32 us -> none
    pallas_call x1, Pallas kernels: 31.1 us -> 31.7 us  [local(): pl.pallas_call(functools.partial(exchange, n_tm, n_space, n_spin), out_sh...]
where the time goes in v4:
time: 33.8 us; the launch traced here: 33.7 us
  Pallas kernels  33.7 us (100%)
    pallas_call x1, Pallas kernels, local(): pl.pallas_call(functools.partial(exchange, n_tm, n_space, n_spin), out_sh...  31.7 us
    pallas_call x1, Pallas kernels, local(): pl.pallas_call(functools.partial(finish, n_tm), out_shape=jax.ShapeDtypeS...  1.96 us

profile of v4, /device:TPU:0, one launch (start us, length us, event | category | flops | bytes accessed | tf_op | source)
XLA Modules:
  0.0 33.7 jit_solution(3065250985396042409)
XLA Ops:
  0.0 31.7 %exchange_and_multiply.1 = (f32[2,4,1,2,128,256]{5,4,3,2,1,0:T(8,128)S(1)}, bf16[4,256,256]{2,1,0:T(8,128)(2,1)S(1)}, bf16[4,256,256]{2,1,0:T(8,128)(2,1)S(1)}, ...) custom-call(f32[2,1,3,128,256]{4,3,2,1,0:T(8,128)} %vec_hbm.1, f32[2,3,1,3,128,256]{5,4,3,2,1,0:T(8,128)} %dis_hbm.1, ...), custom_call_target="tpu_custom_call" | custom-call | tf_op jit(solution)/shard_map/exchange_and_multiply/pallas_call | solution.py:339
  31.7 2.0 %last_block.1 = f32[2,4,1,2,128,256]{5,4,3,2,1,0:T(8,128)} custom-call(f32[2,4,1,2,128,256]{5,4,3,2,1,0:T(8,128)S(1)} %get-tuple-element.10.y_ref, bf16[4,256,256]{2,1,0:T(8,128)(2,1)S(1)} %get-tuple-element.11.elem_h, bf16[4,256,256]{2,1,0:T(8,128)(2,1)S(1)} %get-tuple-element.12.elem_l, bf16[4,2,256,128]{3,2,1,0:T(8,128)(2,1)S(1)} %get-tuple-element.13.last_h, ...), custom_call_target="tpu_custom_call" | custom-call | tf_op jit(solution)/shard_map/last_block/pallas_call | solution.py:380

commit v5 on v3

--- a/solution.py
+++ b/solution.py
@@ -214,12 +214,9 @@
     for copy in tables + [own]:
         copy.wait()
     take_x(0)
-    for d in [0] + order:
+    for d in [0] + straight:
         from_sibling[0, d].wait_recv()
         mix(0, d)
-    for e in range(1, n_space):
-        from_sibling[e, 0].wait_recv()
-        mix(e, 0)
 
     for copy in to_x.values():
         copy.wait_recv()
@@ -243,6 +240,12 @@
         elem[c, o, 1] = e_im
     elem_copy = send(elem.at[c], elem.at[c], e_send.at[0], e_recv.at[0], sibling)
     k_rows = n_spin * rows
+    for e in range(1, n_space):
+        from_sibling[e, 0].wait_recv()
+        mix(e, 0)
+    for d in order[1:]:
+        from_sibling[0, d].wait_recv()
+        mix(0, d)
     elem_copy.wait_recv()
     for o in range(n_op):
         for reim in range(2):
@@ -261,7 +264,7 @@
         held = (lane >= place * cols) & (lane < (place + 1) * cols)
         columns = pl.ds(pl.multiple_of(owner // per_tile * tile, tile), tile)
 
-        for o in range(n_op):
+        def one(o, carry):
             for e in fresh:
                 mix_one(e, d, o)
             right = [
@@ -278,6 +281,13 @@
                     out_ref[reim, o, 0, a, :, columns] = jnp.where(
                         held, moved, out_ref[reim, o, 0, a, :, columns]
                     )
+            return carry
+
+        if d in (0, order[0], *order[-2:]):
+            for o in range(n_op):
+                one(o, 0)
+        else:
+            lax.fori_loop(0, n_op, one, 0)
 
     multiply(0)
     before = None

time: 32.6 us -> 31.5 us (0.966)
  Pallas kernels: 31.1 us -> 30.1 us
    pallas_call x1, Pallas kernels: 31.1 us -> 30.1 us  [local(): pl.pallas_call(functools.partial(exchange, n_tm, n_space, n_spin), out_sh...]
where the time goes in v5:
time: 31.5 us; the launch traced here: 31.4 us
  Pallas kernels  30.1 us (96%)
  local copies, waits for them, and re-layouts  1.32 us (4%)
    pallas_call x1, Pallas kernels, local(): pl.pallas_call(functools.partial(exchange, n_tm, n_space, n_spin), out_sh...  30.1 us
    unnamed x1, local copies, waits for them, and re-layouts  1.32 us

profile of v5, /device:TPU:0, one launch (start us, length us, event | category | flops | bytes accessed | tf_op | source)
XLA Modules:
  0.0 31.4 jit_solution(5041729892757981858)
XLA Ops:
  0.0 30.1 %exchange_and_multiply.1 = f32[2,4,1,2,128,256]{5,4,3,2,1,0:T(8,128)S(1)} custom-call(f32[2,1,3,128,256]{4,3,2,1,0:T(8,128)} %vec_hbm.1, f32[2,3,1,3,128,256]{5,4,3,2,1,0:T(8,128)} %dis_hbm.1, f32[2,4,2,64,128]{4,3,2,1,0:T(8,128)} %bitcast.1, f32[2,4,4,4]{3,2,1,0:T(4,128)} %gamma_hbm.1, s32[4,4,4]{2,1,0:T(4,128)} %pattern_hbm.1, s32[4]{0:T(128)} %directions_hbm.1, ...), custom_call_target="tpu_custom_call" | custom-call | tf_op jit(solution)/shard_map/exchange_and_multiply/pallas_call | solution.py:321
  30.1 1.3 %copy.9 = f32[2,4,1,2,128,256]{5,4,3,2,1,0:T(8,128)} copy(f32[2,4,1,2,128,256]{5,4,3,2,1,0:T(8,128)S(1)} %exchange_and_multiply.1) | data formatting | bytes 4194304
